TPU v7x, 32 devices: a whole 2x2x4 slice. The times are simulated.
32 devices in a mesh: ctx: 16 (over z, y, x), head: 2 (over core).
Axes of the slice: x: 2, y: 2, z: 4, core: 2. Of those that a mesh axis runs over, the one named last changes fastest.
Arguments:
- q_self: bfloat16 [2048, 1024], P('ctx', 'head'), may hold values from -6 to 6
- k_self: bfloat16 [2048, 1024], P('ctx', 'head'), may hold values from -6 to 6
- v_self: bfloat16 [2048, 1024], P('ctx', 'head'), may hold values from -6 to 6
- q_cross: bfloat16 [2048, 1024], P('ctx', 'head'), may hold values from -6 to 6
- n_keys: bfloat16 [8192, 1024], P('ctx', 'head'), may hold values from -6 to 6
- n_values: bfloat16 [8192, 1024], P('ctx', 'head'), may hold values from -6 to 6
- d_cross: bfloat16 [2048, 1024], P('ctx', 'head'), may hold values from -16 to 16
Outputs:
- self_out: bfloat16 [2048, 1024], P('ctx', 'head')
- cross_out: bfloat16 [2048, 1024], P('ctx', 'head')
- d_query: bfloat16 [2048, 1024], P('ctx', 'head')
- d_keys: bfloat16 [8192, 1024], P('ctx', 'head')
- d_values: bfloat16 [8192, 1024], P('ctx', 'head')
All inputs are finite; a program needn't handle non-finite values.
Results may differ from a plain program's by a relative error of at most 0.012.
Values may be sent and summed in bfloat16 or wider, within the bound.
A program may use at most 128 MiB of HBM per device.

v0:
```python
import math

import jax
import jax.numpy as jnp
from jax import lax
from jax.sharding import PartitionSpec as P

HD = 128
SPAN = 64


def from_behind(block, axis, distance):
    devices = range(lax.axis_size(axis))
    route = [(i - distance, i) for i in devices if i - distance in devices]
    return lax.ppermute(block, axis, route)


def attend_block(folded, keys_block, values_block, key_first, queries, positions):
    running_max, running_sum, accumulated = folded
    scores = jnp.einsum("rhd,khd->hrk", queries, keys_block, preferred_element_type=jnp.float32) * (
        1.0 / math.sqrt(HD)
    )
    key_positions = key_first + jnp.arange(keys_block.shape[0], dtype=jnp.int32)
    visible = (key_positions[None, :] <= positions[:, None])[None]
    masked = jnp.where(visible, scores, jnp.float32(-1e30))
    new_max = jnp.maximum(running_max, jnp.max(masked, axis=2))
    weights = jnp.where(visible, jnp.exp(masked - new_max[:, :, None]), jnp.float32(0.0))
    rescale = jnp.exp(running_max - new_max)
    new_sum = running_sum * rescale + jnp.sum(weights, axis=2)
    product = jnp.einsum(
        "hrk,khd->hrd",
        weights.astype(jnp.bfloat16),
        values_block,
        preferred_element_type=jnp.float32,
    )
    return (new_max, new_sum, accumulated * rescale[:, :, None] + product)


def self_attention(groups, keys_local, values_local):
    column_count = keys_local.shape[1]
    head_count = column_count // HD
    prepared = []
    for queries_flat, positions in groups:
        row_count = queries_flat.shape[0]
        prepared.append(
            (queries_flat.reshape(row_count, head_count, HD), positions, jnp.max(positions))
        )
    initial = tuple(
        (
            (
                jnp.full((head_count, entry[0].shape[0]), -1e30, jnp.float32),
                jnp.zeros((head_count, entry[0].shape[0]), jnp.float32),
                jnp.zeros((head_count, entry[0].shape[0], HD), jnp.float32),
            )
            for entry in prepared
        )
    )
    folded = initial
    keys_piece = lax.all_gather(keys_local, "ctx", axis=0, tiled=True)
    values_piece = lax.all_gather(values_local, "ctx", axis=0, tiled=True)
    piece_rows = keys_piece.shape[0]
    block_rows = 512
    block_count = piece_rows // block_rows
    key_blocks = keys_piece.reshape(block_count, block_rows, head_count, HD)
    value_blocks = values_piece.reshape(block_count, block_rows, head_count, HD)

    def visit(inner, items):
        keys_block, values_block, block_index = items
        key_first = block_index * block_rows
        updated = []
        for state, entry in zip(inner, prepared):
            queries, positions, last_position = entry

            def update(current, queries=queries, positions=positions):
                return attend_block(
                    current, keys_block, values_block, key_first, queries, positions
                )

            def unchanged(current):
                return current

            updated.append(lax.cond(key_first <= last_position, update, unchanged, state))
        return (tuple(updated), None)

    folded, unused = lax.scan(
        visit, folded, (key_blocks, value_blocks, jnp.arange(block_count, dtype=jnp.int32))
    )
    outputs = []
    for state in folded:
        running_max, running_sum, accumulated = state
        mixed = accumulated / running_sum[:, :, None]
        row_count = mixed.shape[1]
        outputs.append(
            mixed.transpose(1, 0, 2).reshape(row_count, column_count).astype(jnp.bfloat16)
        )
    return outputs


def cross_attention(q_cross, n_keys, n_values, d_cross):
    row_count, column_count = q_cross.shape
    head_count = column_count // HD
    lag_rows = SPAN - 1
    scale_factor = 1.0 / math.sqrt(HD)
    incoming = from_behind(q_cross[:lag_rows], "ctx", -1)
    shifted = jnp.concatenate([q_cross[lag_rows:], incoming], axis=0)
    span_count = row_count // SPAN
    neighbour_rows = n_keys.shape[0] // span_count
    queries = shifted.reshape(span_count, SPAN, head_count, HD)
    neighbour_keys = n_keys.reshape(span_count, neighbour_rows, head_count, HD)
    neighbour_values = n_values.reshape(span_count, neighbour_rows, head_count, HD)
    grad_rows = d_cross.reshape(span_count, SPAN, head_count, HD)
    scores = (
        jnp.einsum("crhd,ckhd->chrk", queries, neighbour_keys, preferred_element_type=jnp.float32)
        * scale_factor
    )
    row_max = jnp.max(scores, axis=3, keepdims=True)
    weights = jnp.exp(scores - row_max)
    probs = weights / jnp.sum(weights, axis=3, keepdims=True)
    probs_low = probs.astype(jnp.bfloat16)
    attended = jnp.einsum(
        "chrk,ckhd->crhd", probs_low, neighbour_values, preferred_element_type=jnp.float32
    )
    cross_out = attended.reshape(row_count, column_count).astype(jnp.bfloat16)
    grad_probs = jnp.einsum(
        "crhd,ckhd->chrk", grad_rows, neighbour_values, preferred_element_type=jnp.float32
    )
    centre = jnp.sum(grad_probs * probs, axis=3, keepdims=True)
    grad_scores = (probs * (grad_probs - centre) * scale_factor).astype(jnp.bfloat16)
    grad_source = jnp.einsum(
        "chrk,ckhd->crhd", grad_scores, neighbour_keys, preferred_element_type=jnp.float32
    )
    grad_source = grad_source.reshape(row_count, column_count).astype(jnp.bfloat16)
    grad_keys = jnp.einsum(
        "chrk,crhd->ckhd", grad_scores, queries, preferred_element_type=jnp.float32
    ).reshape(n_keys.shape)
    grad_values = jnp.einsum(
        "chrk,crhd->ckhd", probs_low, grad_rows, preferred_element_type=jnp.float32
    ).reshape(n_values.shape)
    carried = from_behind(grad_source[row_count - lag_rows :], "ctx", 1)
    d_query = jnp.concatenate([carried, grad_source[: row_count - lag_rows]], axis=0)
    squares = jnp.sum(grad_keys * grad_keys) + jnp.sum(grad_values * grad_values)
    overall = lax.psum(squares, ("ctx", "head"))
    element_count = 2.0 * grad_keys.size * lax.axis_size("ctx") * lax.axis_size("head")
    factor = lax.rsqrt(overall / element_count + 1e-06)
    d_keys = (grad_keys * factor).astype(jnp.bfloat16)
    d_values = (grad_values * factor).astype(jnp.bfloat16)
    return (cross_out, d_query, d_keys, d_values)


def body(q_self, k_self, v_self, q_cross, n_keys, n_values, d_cross):
    row_count = q_self.shape[0]
    device_index = lax.axis_index("ctx")
    first_row = device_index * row_count
    own_positions = first_row + jnp.arange(row_count, dtype=jnp.int32)
    self_out = self_attention([(q_self, own_positions)], k_self, v_self)[0]
    cross_out, d_query, d_keys, d_values = cross_attention(q_cross, n_keys, n_values, d_cross)
    return (self_out, cross_out, d_query, d_keys, d_values)


def solution(mesh):
    in_specs = (
        P("ctx", "head"),
        P("ctx", "head"),
        P("ctx", "head"),
        P("ctx", "head"),
        P("ctx", "head"),
        P("ctx", "head"),
        P("ctx", "head"),
    )
    out_specs = (
        P("ctx", "head"),
        P("ctx", "head"),
        P("ctx", "head"),
        P("ctx", "head"),
        P("ctx", "head"),
    )
    return jax.shard_map(body, mesh=mesh, in_specs=in_specs, out_specs=out_specs, check_vma=False)
```

profile of v0, /device:TPU:30, one launch (start us, length us, event | category | flops | bytes accessed | tf_op | source)
XLA Modules:
  0.0 164.6 jit_solution(2001189079652478274)
XLA Ops:
  7.2 0.7 all-gather.3.cloned.1.call-update
  8.0 0.7 all-gather.5.cloned.1.call-update
  8.7 0.8 slice.13
  9.5 2.4 %collective-permute-start = (bf16[63,512]{1,0:T(8,128)(2,1)S(1)}, bf16[63,512]{1,0:T(8,128)(2,1)S(1)}, u32[]{:S(2)}, u32[]{:S(2)}) collective-permute-start(bf16[63,512]{1,0:T(8,128)(2,1)S(1)} %slice.13), channel_id=1, source_target_pairs={{2,0},{4,2},{6,4},{8,6},{10,8},{12,10},{14,12},{16,14},{18,16},{20... | collective-permute-start | bytes 193544 | tf_op jit(solution)/shard_map/ppermute | solution.py:15
  12.0 0.9 reshape.90
  12.9 1.2 reshape.89
  14.4 0.7 add_reduce_fusion
  15.9 1.4 fusion.54
  17.3 2.5 %fusion.26 = bf16[2,64,4,128]{3,1,2,0:T(8,128)(2,1)S(1)} fusion(f32[2,4,64,256]{3,2,1,0:T(8,128)S(1)} %fusion.34, bf16[2,256,4,128]{3,2,1,0:T(4,128)(2,1)S(1)} %reshape.88, f32[2,4,64,256]{3,2,1,0:T(8,128)S(1)} %get-tuple-element.207, f32[2,4,64]{2,1,0:T(4,128)S(1)} %get-tuple-element.206), kind=kOutput, calls=%fused_computation.35 | convolution fusion | flops 34538240 | bytes 1705984 | tf_op jit(solution)/shard_map/chrk,ckhd->crhd/dot_general | solution.py:129
  20.6 1.9 %multiply_reduce_fusion = (f32[]{:T(128)}, f32[2,4,256,128]{3,2,1,0:T(8,128)S(1)}) fusion(bf16[2,64,4,128]{3,2,1,0:T(4,128)(2,1)S(1)} %reshape.90, f32[2,4,64]{2,1,0:T(4,128)S(1)} %get-tuple-element.206, f32[2,4,64,256]{3,2,1,0:T(8,128)S(1)} %convolution_multiply_fusion.1), kind=kOutput, calls=%fused_computation.39 | convolution fusion | flops 34472704 | bytes 1705988 | tf_op jit(solution)/shard_map/chrk,crhd->ckhd/dot_general | solution.py:136
  22.5 4.8 %multiply_reduce_fusion.1 = (f32[]{:T(128)}, f32[2,4,128,256]{3,2,1,0:T(8,128)S(1)}) fusion(f32[2,4,64,256]{3,2,1,0:T(8,128)} %copy-done.1, f32[2,4,64,256]{3,2,1,0:T(8,128)} %copy-done.2, f32[2,4,64]{2,1,0:T(4,128)S(1)} %get-tuple-element.206, bf16[2,64,4,128]{3,2,1,0:T(4,128)(2,1)S(1)} %reshape.87), kind=kOutput, calls=%fused_computation.40 | convolution fusion | flops 34996992 | bytes 2230276 | tf_op jit(solution)/shard_map/chrk,crhd->ckhd/dot_general | solution.py:133
  28.5 1.3 collective-permute-start.1
  29.8 43.6 %psum.7 = f32[]{:T(128)} all-reduce(f32[]{:T(128)S(6)} %add.41), channel_id=1, replica_groups=mesh['ctx'=16,'head'=2] {'ctx','head'}, use_global_device_ids=true, to_apply=%region_12.13 | all-reduce | flops 1 | bytes 8 | tf_op jit(solution)/shard_map/psum | solution.py:142
  75.0 1.1 copy_bitcast_fusion
  76.1 1.0 fusion.25
  77.2 0.7 copy.70
  77.9 0.7 pad_maximum_fusion.1
  78.6 4.0 %reshape.84 = bf16[4,512,4,128]{3,2,1,0:T(4,128)(2,1)} reshape(bf16[2048,512]{1,0:T(8,128)(2,1)} %all-gather.3.cloned.1.call-done) | data formatting | bytes 4194304 | tf_op jit(solution)/shard_map/reshape | solution.py:64
  82.6 2.0 %copy.22 = bf16[4,512,4,128]{3,1,2,0:T(8,128)(2,1)S(1)} copy(bf16[4,512,4,128]{3,2,1,0:T(4,128)(2,1)} %reshape.84) | data formatting | bytes 4194304
  84.6 48.3 %all-gather.5.cloned.1.call-done = bf16[2048,512]{1,0:T(8,128)(2,1)} async-done(((bf16[128,512]{1,0:T(8,128)(2,1)}), bf16[2048,512]{1,0:T(8,128)(2,1)}) %all-gather.5.cloned.1.call-update) | async-done | bytes 2097168 | tf_op jit(solution)/shard_map/all_gather | solution.py:60
  132.9 4.0 %reshape.86 = bf16[4,512,4,128]{3,2,1,0:T(4,128)(2,1)} reshape(bf16[2048,512]{1,0:T(8,128)(2,1)} %all-gather.5.cloned.1.call-done) | data formatting | bytes 4194304 | tf_op jit(solution)/shard_map/reshape | solution.py:65
  136.9 3.4 %copy.24 = bf16[4,512,4,128]{3,1,2,0:T(8,128)(2,1)} copy(bf16[4,512,4,128]{3,2,1,0:T(4,128)(2,1)} %reshape.86) | data formatting | bytes 4194304
  140.3 16.7 %while.15 = (s32[]{:T(128)}, f32[4,128]{1,0:T(4,128)S(1)}, f32[4,128]{1,0:T(4,128)S(1)}, f32[4,128,128]{2,1,0:T(8,128)S(1)}, s32[4]{0:T(128)S(1)}, /*index=5*/s3...) while((s32[]{:T(128)}, f32[4,128]{1,0:T(4,128)S(1)}, ...), condition=%wide.region_6.7_spmd.clone, body=%wide.region_1.6_spmd.clone.sunk | while | flops 136775296 | bytes 5151543 | solution.py:85
  142.1 2.3 %conditional.3 = ((f32[4,128]{1,0:T(4,128)S(1)}, f32[4,128]{1,0:T(4,128)S(1)}, f32[4,128,128]{2,1,0:T(8,128)S(1)})) conditional(s32[]{:T(128)} %convert_element_type.109, (f32[4,128]{1,0:T(4,128)S(1)}, f32[4,128]{1,0:T(4,128)S(1)}, f32[4,128,128]{2,1,0:T(8,128)S(1)}) %tuple.47, (s32[]{:T(128)}, s32[]{:T(128)}, bf16[4,512,4,128]{3,1,2,0:T(8,128)(2,1)S(1)}, ...), branch_computations={%region_2.2_spmd, %region_3.5_spmd} | conditional | flops 136775296 | bytes 5150764 | solution.py:82
  142.9 1.5 convolution_add_fusion
  146.3 2.3 %conditional.3 = ((f32[4,128]{1,0:T(4,128)S(1)}, f32[4,128]{1,0:T(4,128)S(1)}, f32[4,128,128]{2,1,0:T(8,128)S(1)})) conditional(s32[]{:T(128)} %convert_element_type.109, (f32[4,128]{1,0:T(4,128)S(1)}, f32[4,128]{1,0:T(4,128)S(1)}, f32[4,128,128]{2,1,0:T(8,128)S(1)}) %tuple.47, (s32[]{:T(128)}, s32[]{:T(128)}, bf16[4,512,4,128]{3,1,2,0:T(8,128)(2,1)S(1)}, ...), branch_computations={%region_2.2_spmd, %region_3.5_spmd} | conditional | flops 136775296 | bytes 5150764 | solution.py:82
  147.1 1.5 convolution_add_fusion
  150.5 2.3 %conditional.3 = ((f32[4,128]{1,0:T(4,128)S(1)}, f32[4,128]{1,0:T(4,128)S(1)}, f32[4,128,128]{2,1,0:T(8,128)S(1)})) conditional(s32[]{:T(128)} %convert_element_type.109, (f32[4,128]{1,0:T(4,128)S(1)}, f32[4,128]{1,0:T(4,128)S(1)}, f32[4,128,128]{2,1,0:T(8,128)S(1)}) %tuple.47, (s32[]{:T(128)}, s32[]{:T(128)}, bf16[4,512,4,128]{3,1,2,0:T(8,128)(2,1)S(1)}, ...), branch_computations={%region_2.2_spmd, %region_3.5_spmd} | conditional | flops 136775296 | bytes 5150764 | solution.py:82
  151.2 1.5 convolution_add_fusion
  154.7 2.3 %conditional.3 = ((f32[4,128]{1,0:T(4,128)S(1)}, f32[4,128]{1,0:T(4,128)S(1)}, f32[4,128,128]{2,1,0:T(8,128)S(1)})) conditional(s32[]{:T(128)} %convert_element_type.109, (f32[4,128]{1,0:T(4,128)S(1)}, f32[4,128]{1,0:T(4,128)S(1)}, f32[4,128,128]{2,1,0:T(8,128)S(1)}) %tuple.47, (s32[]{:T(128)}, s32[]{:T(128)}, bf16[4,512,4,128]{3,1,2,0:T(8,128)(2,1)S(1)}, ...), branch_computations={%region_2.2_spmd, %region_3.5_spmd} | conditional | flops 136775296 | bytes 5150764 | solution.py:82
  155.4 1.5 convolution_add_fusion
  157.0 0.8 copy_bitcast_fusion.4
  (76 shorter events, 8.2 us)
Async XLA Ops:
  7.2 7.2 %copy-start.3 = (bf16[128,512]{1,0:T(8,128)(2,1)S(1)}, bf16[128,512]{1,0:T(8,128)(2,1)}, u32[]{:S(2)}) copy-start(bf16[128,512]{1,0:T(8,128)(2,1)} %param.14) | copy-start | bytes 393220
  7.2 7.9 %copy-start.4 = (bf16[128,512]{1,0:T(8,128)(2,1)S(1)}, bf16[128,512]{1,0:T(8,128)(2,1)}, u32[]{:S(2)}) copy-start(bf16[128,512]{1,0:T(8,128)(2,1)} %param.11) | copy-start | bytes 393220
  7.2 8.2 %copy-start = (bf16[512,512]{1,0:T(8,128)(2,1)S(1)}, bf16[512,512]{1,0:T(8,128)(2,1)}, u32[]{:S(2)}) copy-start(bf16[512,512]{1,0:T(8,128)(2,1)} %param.15) | copy-start | bytes 1572868
  7.2 71.4 %all-gather.3.cloned.1.call-start = ((), (), s32[]{:S(2)}) async-start(), calls=%async_computation | async-start | bytes 2228224 | tf_op jit(solution)/shard_map/all_gather | solution.py:59
  7.9 125.0 %all-gather.5.cloned.1.call-start = ((), (), s32[]{:S(2)}) async-start(), calls=%async_computation.1 | async-start | bytes 2228224 | tf_op jit(solution)/shard_map/all_gather | solution.py:60
  9.5 6.0 %collective-permute-start = (bf16[63,512]{1,0:T(8,128)(2,1)S(1)}, bf16[63,512]{1,0:T(8,128)(2,1)S(1)}, u32[]{:S(2)}, u32[]{:S(2)}) collective-permute-start(bf16[63,512]{1,0:T(8,128)(2,1)S(1)} %slice.13), channel_id=1, source_target_pairs={{2,0},{4,2},{6,4},{8,6},{10,8},{12,10},{14,12},{16,14},{18,16},{20... | collective-permute-start | bytes 193544 | tf_op jit(solution)/shard_map/ppermute | solution.py:15
  14.4 2.9 %copy-start.1 = (f32[2,4,64,256]{3,2,1,0:T(8,128)}, f32[2,4,64,256]{3,2,1,0:T(8,128)S(1)}, u32[]{:S(2)}) copy-start(f32[2,4,64,256]{3,2,1,0:T(8,128)S(1)} %fusion.34) | copy-start | bytes 1572868
  17.3 3.3 %copy-start.2 = (f32[2,4,64,256]{3,2,1,0:T(8,128)}, f32[2,4,64,256]{3,2,1,0:T(8,128)S(1)}, u32[]{:S(2)}) copy-start(f32[2,4,64,256]{3,2,1,0:T(8,128)S(1)} %get-tuple-element.207) | copy-start | bytes 1572868
  28.5 49.4 %collective-permute-start.1 = (bf16[63,512]{1,0:T(8,128)(2,1)}, bf16[63,512]{1,0:T(8,128)(2,1)S(1)}, u32[]{:S(2)}, u32[]{:S(2)}) collective-permute-start(bf16[63,512]{1,0:T(8,128)(2,1)} %slice.16), channel_id=1, source_target_pairs={{0,2},{2,4},{4,6},{6,8},{8,10},{10,12},{12,14},{14,16},{16,18},{18... | collective-permute-start | bytes 193544 | tf_op jit(solution)/shard_map/ppermute | solution.py:15
Sparse Core Ops, SparseCore 0:
  10.8 59.9 all-gather.2
  73.5 59.3 all-gather.4
where the time goes:
time: 166 us; the launch traced here: 165 us
  waiting for transfers between devices  49.7 us (30%)
  blocking collectives  43.6 us (26%)
  local copies, waits for them, and re-layouts  22.5 us (14%)
  matrix products  18.1 us (11%)
  between operations  16.2 us (10%)
  loops' own time  5.39 us (3%)
  other arithmetic  5.25 us (3%)
  starting transfers between devices  3.8 us (2%)
    all_gather x1, waiting for transfers between devices, self_attention(): values_piece = lax.all_gather(values_local, 'ctx', axis=0, tiled=True)  48.3 us
    psum x1, blocking collectives, cross_attention(): overall = lax.psum(squares, ('ctx', 'head'))  43.6 us
    unnamed x16, local copies, waits for them, and re-layouts  6.36 us
    dot_general x4, matrix products, attend_block(): jnp.einsum('hrk,khd->hrd', weights.astype(jnp.bfloat16), values_block, pr...  6.07 us
    another operation x1, loops' own time, self_attention(): lax.scan(visit, folded, (key_blocks, value_blocks, jnp.arange(block_count...  5.16 us
    dot_general x1, matrix products, cross_attention(): jnp.einsum('chrk,crhd->ckhd', grad_scores, queries, preferred_element_typ...  4.77 us
    reshape x1, local copies, waits for them, and re-layouts, self_attention(): value_blocks = values_piece.reshape(block_count, block_rows, head_count, HD)  3.98 us
    reshape x1, local copies, waits for them, and re-layouts, self_attention(): key_blocks = keys_piece.reshape(block_count, block_rows, head_count, HD)  3.97 us
  transfers between devices with their start and end apart: 4, of which 1 were waited for; matrix products, arithmetic and copies ran while one was open for 16% of the time, Pallas kernels for 0%

commit v1 on v0

v1 whole, which is shorter than its diff:
```python
import functools
import math

import jax
import jax.numpy as jnp
from jax import lax
from jax.experimental import pallas as pl
from jax.experimental.pallas import tpu as pltpu
from jax.sharding import PartitionSpec as P

HD = 128
SPAN = 64
LAG = SPAN - 1
TAIL = 16
F32 = jnp.float32
BF16 = jnp.bfloat16
NEG = -1e30


def dot(a, b, dims):
    return lax.dot_general(a, b, (dims, ((), ())), preferred_element_type=F32)


def kernel(
    nctx, nhead, group, total_elements,
    q_self, k_self, v_self, q_cross, n_keys, n_values, d_cross,
    self_out, cross_out, d_query, d_keys, d_values,
    kbuf, vbuf, qbuf, osend, orecv, own_o, own_lse,
    qc, nk, nv, dc, shifted, gsrc, cross, dq, gk, gv, dkb, dvb, so,
    sq1, sq2,
    load_sem, out_sem, kv_s, kv_r, q_s, q_r, o_s, o_r, edge_s, edge_r,
    sq1_s, sq1_r, sq2_s, sq2_r,
):
    groups = nctx // group
    rows, cols = q_self.shape
    heads = cols // HD
    nrows = n_keys.shape[0]
    scale = 1.0 / math.sqrt(HD)
    me = lax.axis_index("ctx")
    my_head = lax.axis_index("head")
    hi, lo = me // group, lax.rem(me, group)
    has_next = me < nctx - 1
    has_prev = me > 0

    def hcols(h):
        return pl.ds(pl.multiple_of(h * HD, HD), HD)

    loads = [
        pltpu.make_async_copy(q_cross, qc.at[pl.ds(0, rows)], load_sem.at[0]),
        pltpu.make_async_copy(n_keys, nk, load_sem.at[1]),
        pltpu.make_async_copy(n_values, nv, load_sem.at[2]),
        pltpu.make_async_copy(d_cross, dc, load_sem.at[3]),
        pltpu.make_async_copy(k_self, kbuf.at[lo], load_sem.at[4]),
        pltpu.make_async_copy(v_self, vbuf.at[lo], load_sem.at[5]),
        pltpu.make_async_copy(q_self, qbuf.at[0], load_sem.at[6]),
    ]
    for copy in loads:
        copy.start()

    barrier = pltpu.get_barrier_semaphore()

    def greet(ctx, head):
        pl.semaphore_signal(
            barrier, inc=1, device_id=(ctx, head), device_id_type=pl.DeviceIdType.MESH
        )

    def plane_peer(dl, dh):
        return hi * group + lax.rem(lo + dl, group), lax.rem(my_head + dh, nhead)

    plane_offsets = [(a, b) for a in range(group) for b in range(nhead) if a or b]
    for dl, dh in plane_offsets:
        greet(*plane_peer(dl, dh))
    for d in range(1, groups):
        greet(lax.rem(hi + d, groups) * group + lo, my_head)
    edge_up = jnp.logical_and(lo == group - 1, has_next)
    edge_down = jnp.logical_and(lo == 0, has_prev)

    @pl.when(edge_up)
    def _():
        greet(me + 1, my_head)

    @pl.when(edge_down)
    def _():
        greet(me - 1, my_head)

    pl.semaphore_wait(
        barrier,
        len(plane_offsets) + groups - 1
        + edge_up.astype(jnp.int32) + edge_down.astype(jnp.int32),
    )

    def remote(src, dst, send, recv, ctx, head=None):
        return pltpu.make_async_remote_copy(
            src_ref=src, dst_ref=dst, send_sem=send, recv_sem=recv,
            device_id=(ctx, my_head if head is None else head),
            device_id_type=pl.DeviceIdType.MESH,
        )

    def edge_query():
        return remote(
            q_cross.at[pl.ds(0, SPAN)], qc.at[pl.ds(rows, SPAN)],
            edge_s.at[0], edge_r.at[0], jnp.maximum(me - 1, 0),
        )

    def edge_grad():
        return remote(
            gsrc.at[pl.ds(rows, SPAN)], gsrc.at[pl.ds(0, SPAN)],
            edge_s.at[1], edge_r.at[1], jnp.minimum(me + 1, nctx - 1),
        )

    @pl.when(has_prev)
    def _():
        edge_query().start()

    def kv_copy(d, h, which, slot):
        src, buf = (k_self, kbuf) if which == 0 else (v_self, vbuf)
        return remote(
            src.at[:, hcols(h)], buf.at[slot, :, hcols(h)],
            kv_s.at[d - 1, h, which], kv_r.at[d - 1, h, which],
            hi * group + lax.rem(lo + d, group),
        )

    def q_copy(d, h):
        return remote(
            q_self.at[:, hcols(h)], qbuf.at[d, :, hcols(h)],
            q_s.at[d - 1, h], q_r.at[d - 1, h],
            jnp.maximum(hi - d, 0) * group + lo,
        )

    def o_copy(d, h):
        return remote(
            osend.at[d - 1, h], orecv.at[d - 1, h],
            o_s.at[d - 1, h], o_r.at[d - 1, h],
            jnp.minimum(hi + d, groups - 1) * group + lo,
        )

    @pl.loop(0, heads)
    def _(h):
        for d in range(1, group):
            kv_copy(d, h, 0, lo).start()
            kv_copy(d, h, 1, lo).start()

        @pl.loop(1, groups)
        def _(d):
            @pl.when(hi >= d)
            def _():
                q_copy(d, h).start()

    for copy in loads[:4]:
        copy.wait()

    @pl.when(has_next)
    def _():
        edge_query().wait_recv()

    @pl.when(jnp.logical_not(has_next))
    def _():
        qc[rows:, :] = jnp.zeros((SPAN, cols), BF16)

    row_id = lax.broadcasted_iota(jnp.int32, (rows, rows + SPAN), 0)
    col_id = lax.broadcasted_iota(jnp.int32, (rows, rows + SPAN), 1)
    pick = jnp.where(col_id == row_id + LAG, 1.0, 0.0).astype(BF16)
    shifted[...] = dot(pick, qc[...], ((1,), (0,))).astype(BF16)

    per_span = nrows // (rows // SPAN)
    neighbour = lax.broadcasted_iota(jnp.int32, (nrows, rows), 0)
    query = lax.broadcasted_iota(jnp.int32, (nrows, rows), 1)
    same_span = (neighbour // per_span) == (query // SPAN)

    def cross_head(h, squares):
        c = hcols(h)
        keys, values = nk[:, c], nv[:, c]
        queries, grads = shifted[:, c], dc[:, c]
        st = dot(keys, queries, ((1,), (1,))) * scale
        st = jnp.where(same_span, st, NEG)
        weights = jnp.exp(st - jnp.max(st, axis=0, keepdims=True))
        probs = weights * (1.0 / jnp.sum(weights, axis=0, keepdims=True))
        low = probs.astype(BF16)
        cross[:, c] = dot(low, values, ((0,), (0,))).astype(BF16)
        grad_probs = dot(values, grads, ((1,), (1,)))
        centre = jnp.sum(grad_probs * probs, axis=0, keepdims=True)
        grad_scores = (probs * (grad_probs - centre) * scale).astype(BF16)
        gsrc[SPAN:, c] = dot(grad_scores, keys, ((0,), (0,))).astype(BF16)
        grad_keys = dot(grad_scores, queries, ((1,), (0,)))
        gk[:, c] = grad_keys
        grad_values = dot(low, grads, ((1,), (0,)))
        gv[:, c] = grad_values
        return squares + jnp.sum(
            grad_keys * grad_keys + grad_values * grad_values, axis=0, keepdims=True
        )

    squares = lax.fori_loop(0, heads, cross_head, jnp.zeros((1, HD), F32))
    sq1[0] = jnp.broadcast_to(squares, (8, HD))

    def sq1_copy(dl, dh):
        slot = dl * nhead + dh
        ctx, head = plane_peer(dl, dh)
        return remote(
            sq1.at[0], sq1.at[slot], sq1_s.at[slot], sq1_r.at[slot], ctx, head
        )

    def sq2_copy(d):
        return remote(
            sq2.at[0], sq2.at[d], sq2_s.at[d], sq2_r.at[d],
            lax.rem(hi + d, groups) * group + lo,
        )

    for dl, dh in plane_offsets:
        sq1_copy(dl, dh).start()

    @pl.when(has_next)
    def _():
        edge_grad().start()

    cross_store = pltpu.make_async_copy(cross, cross_out, out_sem.at[0])
    cross_store.start()

    for copy in loads[4:]:
        copy.wait()

    def attend(st, values):
        largest = jnp.max(st, axis=0, keepdims=True)
        weights = jnp.exp(st - largest)
        total = jnp.sum(weights, axis=0, keepdims=True)
        mixed = dot(values, weights.astype(BF16), ((0,), (0,)))
        return mixed * (1.0 / total), largest + jnp.log(total)

    key_id = lax.broadcasted_iota(jnp.int32, (group * rows, rows), 0)
    query_id = lax.broadcasted_iota(jnp.int32, (group * rows, rows), 1)
    tail_id = lax.broadcasted_iota(jnp.int32, (TAIL, HD), 0)

    @pl.loop(0, heads)
    def _(h):
        c = hcols(h)
        for d in range(1, group):
            slot = lax.rem(lo + group - d, group)
            kv_copy(d, h, 0, slot).wait_recv()
            kv_copy(d, h, 1, slot).wait_recv()

        @pl.loop(1, groups)
        def _(step):
            d = groups - step

            @pl.when(hi + d < groups)
            def _():
                q_copy(d, h).wait_recv()
                keys = kbuf[:, :, c].reshape(group * rows, HD)
                values = vbuf[:, :, c].reshape(group * rows, HD)
                mixed, lse = attend(dot(keys, qbuf[d, :, c], ((1,), (1,))) * scale, values)
                osend[d - 1, h, :HD, :] = mixed.astype(BF16)
                high = lse.astype(BF16).astype(F32)
                rest = lse - high
                middle = rest.astype(BF16).astype(F32)
                tail = jnp.where(tail_id == 0, high, jnp.where(tail_id == 1, middle, rest - middle))
                osend[d - 1, h, HD:, :] = tail.astype(BF16)
                o_copy(d, h).start()

        keys = kbuf[:, :, c].reshape(group * rows, HD)
        values = vbuf[:, :, c].reshape(group * rows, HD)
        st = dot(keys, qbuf[0, :, c], ((1,), (1,))) * scale
        st = jnp.where(key_id <= query_id + lo * rows, st, NEG)
        mixed, lse = attend(st, values)
        own_o[h] = mixed
        own_lse[h] = jnp.broadcast_to(lse, (8, HD))

    for dl, dh in plane_offsets:
        sq1_copy(dl, dh).wait_recv()
    sq2[0] = jnp.sum(sq1[...], axis=0)
    for d in range(1, groups):
        sq2_copy(d).start()

    @pl.when(has_prev)
    def _():
        edge_grad().wait_recv()

    @pl.when(jnp.logical_not(has_prev))
    def _():
        gsrc[:SPAN, :] = jnp.zeros((SPAN, cols), BF16)

    back = jnp.where(col_id == row_id + 1, 1.0, 0.0).astype(BF16)
    dq[...] = dot(back, gsrc[...], ((1,), (0,))).astype(BF16)
    query_store = pltpu.make_async_copy(dq, d_query, out_sem.at[1])
    query_store.start()

    for d in range(1, groups):
        sq2_copy(d).wait_recv()
    overall = jnp.sum(jnp.sum(sq2[...], axis=0)[0:1, :], axis=1, keepdims=True)
    factor = lax.rsqrt(overall / total_elements + 1e-06)
    dkb[...] = (gk[...] * factor).astype(BF16)
    keys_store = pltpu.make_async_copy(dkb, d_keys, out_sem.at[2])
    keys_store.start()
    dvb[...] = (gv[...] * factor).astype(BF16)
    values_store = pltpu.make_async_copy(dvb, d_values, out_sem.at[3])
    values_store.start()

    @pl.loop(0, heads)
    def _(h):
        def part(d, state):
            return state

        own_lse[h, 1:2, :] = jnp.ones((1, HD), F32)

        @pl.loop(1, groups)
        def _(d):
            @pl.when(hi >= d)
            def _():
                o_copy(d, h).wait_recv()
                tail = orecv[d - 1, h, HD:, :].astype(F32)
                lse = tail[0:1] + tail[1:2] + tail[2:3]
                before = own_lse[h, 0:1, :]
                top = jnp.maximum(before, lse)
                keep, add = jnp.exp(before - top), jnp.exp(lse - top)
                own_o[h] = own_o[h] * keep + orecv[d - 1, h, :HD, :].astype(F32) * add
                own_lse[h, 0:1, :] = top
                own_lse[h, 1:2, :] = own_lse[h, 1:2, :] * keep + add

        so[:, hcols(h)] = (own_o[h] * (1.0 / own_lse[h, 1:2, :])).T.astype(BF16)

    self_store = pltpu.make_async_copy(so, self_out, out_sem.at[4])
    self_store.start()

    @pl.when(has_prev)
    def _():
        edge_query().wait_send()

    @pl.when(has_next)
    def _():
        edge_grad().wait_send()

    for dl, dh in plane_offsets:
        sq1_copy(dl, dh).wait_send()
    for d in range(1, groups):
        sq2_copy(d).wait_send()

    @pl.loop(0, heads)
    def _(h):
        for d in range(1, group):
            kv_copy(d, h, 0, lo).wait_send()
            kv_copy(d, h, 1, lo).wait_send()

        @pl.loop(1, groups)
        def _(d):
            @pl.when(hi >= d)
            def _():
                q_copy(d, h).wait_send()

            @pl.when(hi + d < groups)
            def _():
                o_copy(d, h).wait_send()

    cross_store.wait()
    query_store.wait()
    keys_store.wait()
    values_store.wait()
    self_store.wait()


def body(nctx, nhead, q_self, k_self, v_self, q_cross, n_keys, n_values, d_cross):
    rows, cols = q_self.shape
    nrows = n_keys.shape[0]
    heads = cols // HD
    group = 4 if nctx % 4 == 0 else nctx
    groups = nctx // group
    far = max(groups - 1, 1)
    dma = pltpu.SemaphoreType.DMA
    spec = pl.BlockSpec(memory_space=pl.ANY)
    small = jax.ShapeDtypeStruct((rows, cols), BF16)
    large = jax.ShapeDtypeStruct((nrows, cols), BF16)
    return pl.pallas_call(
        functools.partial(kernel, nctx, nhead, group, 2.0 * nrows * cols * nctx * nhead),
        out_shape=(small, small, small, large, large),
        in_specs=[spec] * 7,
        out_specs=(spec,) * 5,
        scratch_shapes=[
            pltpu.VMEM((group, rows, cols), BF16),
            pltpu.VMEM((group, rows, cols), BF16),
            pltpu.VMEM((groups, rows, cols), BF16),
            pltpu.VMEM((far, heads, HD + TAIL, rows), BF16),
            pltpu.VMEM((far, heads, HD + TAIL, rows), BF16),
            pltpu.VMEM((heads, HD, rows), F32),
            pltpu.VMEM((heads, 8, rows), F32),
            pltpu.VMEM((rows + SPAN, cols), BF16),
            pltpu.VMEM((nrows, cols), BF16),
            pltpu.VMEM((nrows, cols), BF16),
            pltpu.VMEM((rows, cols), BF16),
            pltpu.VMEM((rows, cols), BF16),
            pltpu.VMEM((rows + SPAN, cols), BF16),
            pltpu.VMEM((rows, cols), BF16),
            pltpu.VMEM((rows, cols), BF16),
            pltpu.VMEM((nrows, cols), F32),
            pltpu.VMEM((nrows, cols), F32),
            pltpu.VMEM((nrows, cols), BF16),
            pltpu.VMEM((nrows, cols), BF16),
            pltpu.VMEM((rows, cols), BF16),
            pltpu.VMEM((group * nhead, 8, HD), F32),
            pltpu.VMEM((groups, 8, HD), F32),
            dma((7,)),
            dma((5,)),
            dma((group - 1, heads, 2)),
            dma((group - 1, heads, 2)),
            dma((far, heads)),
            dma((far, heads)),
            dma((far, heads)),
            dma((far, heads)),
            dma((2,)),
            dma((2,)),
            dma((group * nhead,)),
            dma((group * nhead,)),
            dma((groups,)),
            dma((groups,)),
        ],
        compiler_params=pltpu.CompilerParams(
            collective_id=0, has_side_effects=True, vmem_limit_bytes=40 * 1024 * 1024
        ),
        cost_estimate=pl.CostEstimate(flops=10**9, bytes_accessed=4 * 10**6, transcendentals=10**6),
    )(q_self, k_self, v_self, q_cross, n_keys, n_values, d_cross)


def solution(mesh):
    spec = P("ctx", "head")
    return jax.shard_map(
        functools.partial(body, mesh.shape["ctx"], mesh.shape["head"]),
        mesh=mesh, in_specs=(spec,) * 7, out_specs=(spec,) * 5, check_vma=False,
    )
```

time: 166 us -> 40.4 us (0.24)
  waiting for transfers between devices: 49.7 us -> 0 us
  blocking collectives: 43.6 us -> 0 us
  Pallas kernels: 0 us -> 29.3 us
  matrix products: 18.1 us -> 0 us
  between operations: 16.2 us -> 0.66 us
  local copies, waits for them, and re-layouts: 22.5 us -> 10.1 us
  loops' own time: 5.39 us -> 0 us
  other arithmetic: 5.25 us -> 0 us
  starting transfers between devices: 3.8 us -> 0 us
    all_gather x2 -> x0, waiting for transfers between devices: 48.3 us -> none  [the longest x1 48.3 us: self_attention(): values_piece = lax.all_gather(values_local, 'ctx', axis=0, tiled=True)]
    psum x1 -> x0, blocking collectives: 43.6 us -> none  [cross_attention(): overall = lax.psum(squares, ('ctx', 'head'))]
    pallas_call x0 -> x1, Pallas kernels: none -> 29.3 us  [body(): pl.pallas_call(functools.partial(kernel, nctx, nhead, group, 2.0 * nrows...]
    dot_general x14 -> x0, matrix products: 18.1 us -> none  [the longest x4 6.07 us: attend_block(): jnp.einsum('hrk,khd->hrd', weights.astype(jnp.bfloat16), values_block, pr...]
    reshape x6 -> x0, local copies, waits for them, and re-layouts: 10.2 us -> none  [the longest x1 3.98 us: self_attention(): value_blocks = values_piece.reshape(block_count, block_rows, head_count, HD)]
    another operation x5 -> x0, loops' own time: 5.39 us -> none  [the longest x1 5.16 us: self_attention(): lax.scan(visit, folded, (key_blocks, value_blocks, jnp.arange(block_count...]
    unnamed x16 -> x19, local copies, waits for them, and re-layouts: 6.36 us -> 10.1 us
    ppermute x2 -> x0, starting transfers between devices: 3.72 us -> none  [from_behind(): return lax.ppermute(block, axis, route)]
  transfers between devices with their start and end apart: 4 -> 0, of which waited for: 1 -> 0; matrix products, arithmetic and copies ran while one was open for 16% -> 0% of each run, Pallas kernels for 0% -> 0%
where the time goes in v1:
time: 40.4 us; the launch traced here: 40.1 us
  Pallas kernels  29.3 us (73%)
  local copies, waits for them, and re-layouts  10.1 us (25%)
  between operations  0.66 us (2%)
    pallas_call x1, Pallas kernels, body(): pl.pallas_call(functools.partial(kernel, nctx, nhead, group, 2.0 * nrows...  29.3 us
    unnamed x19, local copies, waits for them, and re-layouts  10.1 us

profile of v1, /device:TPU:30, one launch (start us, length us, event | category | flops | bytes accessed | tf_op | source)
XLA Modules:
  0.0 40.1 jit_solution(13310024980744519264)
XLA Ops:
  0.6 0.0 copy-start
  0.6 1.0 %copy-done = bf16[512,512]{1,0:T(8,128)(2,1)S(1)} copy-done((bf16[512,512]{1,0:T(8,128)(2,1)S(1)}, bf16[512,512]{1,0:T(8,128)(2,1)}, u32[]{:S(2)}) %copy-start) | copy-done | bytes 524312
  1.7 0.0 copy-start.1
  1.7 1.0 %copy-done.1 = bf16[512,512]{1,0:T(8,128)(2,1)S(1)} copy-done((bf16[512,512]{1,0:T(8,128)(2,1)S(1)}, bf16[512,512]{1,0:T(8,128)(2,1)}, u32[]{:S(2)}) %copy-start.1) | copy-done | bytes 524312
  2.7 0.0 copy-start.2
  2.7 0.9 %copy-done.2 = bf16[128,512]{1,0:T(8,128)(2,1)S(1)} copy-done((bf16[128,512]{1,0:T(8,128)(2,1)S(1)}, bf16[128,512]{1,0:T(8,128)(2,1)}, u32[]{:S(2)}) %copy-start.2) | copy-done | bytes 131096
  3.6 0.0 copy-start.3
  3.6 0.9 %copy-done.3 = bf16[128,512]{1,0:T(8,128)(2,1)S(1)} copy-done((bf16[128,512]{1,0:T(8,128)(2,1)S(1)}, bf16[128,512]{1,0:T(8,128)(2,1)}, u32[]{:S(2)}) %copy-start.3) | copy-done | bytes 131096
  4.5 0.0 copy-start.4
  4.5 0.9 %copy-done.4 = bf16[128,512]{1,0:T(8,128)(2,1)S(1)} copy-done((bf16[128,512]{1,0:T(8,128)(2,1)S(1)}, bf16[128,512]{1,0:T(8,128)(2,1)}, u32[]{:S(2)}) %copy-start.4) | copy-done | bytes 131096
  5.4 0.0 copy-start.5
  5.4 0.9 %copy-done.5 = bf16[128,512]{1,0:T(8,128)(2,1)S(1)} copy-done((bf16[128,512]{1,0:T(8,128)(2,1)S(1)}, bf16[128,512]{1,0:T(8,128)(2,1)}, u32[]{:S(2)}) %copy-start.5) | copy-done | bytes 131096
  6.3 0.0 copy-start.6
  6.3 0.9 %copy-done.6 = bf16[128,512]{1,0:T(8,128)(2,1)S(1)} copy-done((bf16[128,512]{1,0:T(8,128)(2,1)S(1)}, bf16[128,512]{1,0:T(8,128)(2,1)}, u32[]{:S(2)}) %copy-start.6) | copy-done | bytes 131096
  7.2 29.3 %shard_map.110 = (bf16[128,512]{1,0:T(8,128)(2,1)S(1)}, bf16[128,512]{1,0:T(8,128)(2,1)S(1)}, bf16[128,512]{1,0:T(8,128)(2,1)S(1)}, bf16[512,512]{1,0:T(8,128)(2,1)S(1)}, bf16[512,512]{1,0:T(8,128)(2,1)S(1)}) custom-call(bf16[128,512]{1,0:T(8,128)(2,1)S(1)} %copy-done.2, bf16[128,512]{1,0:T(8,128)(2,1)S(1)} %copy-done.3, bf16[128,512]{1,0:T(8,128)(2,1)S(1)} %copy-done.4, ...), custom_call_target="tpu_custom_call" | custom-call | flops 1000000000 | bytes 4000000 | tf_op jit(solution)/shard_map/pallas_call | solution.py:369
  36.6 0.7 %copy.17 = bf16[128,512]{1,0:T(8,128)(2,1)} copy(bf16[128,512]{1,0:T(8,128)(2,1)S(1)} %get-tuple-element.10) | data formatting | bytes 262144
  37.2 0.7 %copy.18 = bf16[128,512]{1,0:T(8,128)(2,1)} copy(bf16[128,512]{1,0:T(8,128)(2,1)S(1)} %get-tuple-element.11) | data formatting | bytes 262144
  37.9 0.7 %copy.19 = bf16[128,512]{1,0:T(8,128)(2,1)} copy(bf16[128,512]{1,0:T(8,128)(2,1)S(1)} %get-tuple-element.12) | data formatting | bytes 262144
  38.5 0.8 %copy.20 = bf16[512,512]{1,0:T(8,128)(2,1)} copy(bf16[512,512]{1,0:T(8,128)(2,1)S(1)} %get-tuple-element.13) | data formatting | bytes 1048576
  39.3 0.8 %copy.21 = bf16[512,512]{1,0:T(8,128)(2,1)} copy(bf16[512,512]{1,0:T(8,128)(2,1)S(1)} %get-tuple-element.14) | data formatting | bytes 1048576
Async XLA Ops:
  0.6 1.0 %copy-start = (bf16[512,512]{1,0:T(8,128)(2,1)S(1)}, bf16[512,512]{1,0:T(8,128)(2,1)}, u32[]{:S(2)}) copy-start(bf16[512,512]{1,0:T(8,128)(2,1)} %n_keys.1) | copy-start | bytes 1572868
  1.7 1.0 %copy-start.1 = (bf16[512,512]{1,0:T(8,128)(2,1)S(1)}, bf16[512,512]{1,0:T(8,128)(2,1)}, u32[]{:S(2)}) copy-start(bf16[512,512]{1,0:T(8,128)(2,1)} %n_values.1) | copy-start | bytes 1572868
  2.7 0.9 %copy-start.2 = (bf16[128,512]{1,0:T(8,128)(2,1)S(1)}, bf16[128,512]{1,0:T(8,128)(2,1)}, u32[]{:S(2)}) copy-start(bf16[128,512]{1,0:T(8,128)(2,1)} %q_self.1) | copy-start | bytes 393220
  3.6 0.9 %copy-start.3 = (bf16[128,512]{1,0:T(8,128)(2,1)S(1)}, bf16[128,512]{1,0:T(8,128)(2,1)}, u32[]{:S(2)}) copy-start(bf16[128,512]{1,0:T(8,128)(2,1)} %k_self.1) | copy-start | bytes 393220
  4.5 0.9 %copy-start.4 = (bf16[128,512]{1,0:T(8,128)(2,1)S(1)}, bf16[128,512]{1,0:T(8,128)(2,1)}, u32[]{:S(2)}) copy-start(bf16[128,512]{1,0:T(8,128)(2,1)} %v_self.1) | copy-start | bytes 393220
  5.4 0.9 %copy-start.5 = (bf16[128,512]{1,0:T(8,128)(2,1)S(1)}, bf16[128,512]{1,0:T(8,128)(2,1)}, u32[]{:S(2)}) copy-start(bf16[128,512]{1,0:T(8,128)(2,1)} %q_cross.1) | copy-start | bytes 393220
  6.3 0.9 %copy-start.6 = (bf16[128,512]{1,0:T(8,128)(2,1)S(1)}, bf16[128,512]{1,0:T(8,128)(2,1)}, u32[]{:S(2)}) copy-start(bf16[128,512]{1,0:T(8,128)(2,1)} %d_cross.1) | copy-start | bytes 393220

commit v2 on v1

--- a/solution.py
+++ b/solution.py
@@ -295,9 +295,6 @@
 
     @pl.loop(0, heads)
     def _(h):
-        def part(d, state):
-            return state
-
         own_lse[h, 1:2, :] = jnp.ones((1, HD), F32)
 
         @pl.loop(1, groups)
@@ -355,6 +352,21 @@
     self_store.wait()
 
 
+def write_out(*refs):
+    sources, targets, held = refs[:5], refs[5:10], refs[10:15]
+    in_sem, out_sem = refs[15], refs[16]
+    order = (3, 4, 0, 1, 2)
+    fetch = [pltpu.make_async_copy(sources[i], held[i], in_sem.at[i]) for i in range(5)]
+    store = [pltpu.make_async_copy(held[i], targets[i], out_sem.at[i]) for i in range(5)]
+    for i in order:
+        fetch[i].start()
+    for i in order:
+        fetch[i].wait()
+        store[i].start()
+    for i in order:
+        store[i].wait()
+
+
 def body(nctx, nhead, q_self, k_self, v_self, q_cross, n_keys, n_values, d_cross):
     rows, cols = q_self.shape
     nrows = n_keys.shape[0]
@@ -366,7 +378,7 @@
     spec = pl.BlockSpec(memory_space=pl.ANY)
     small = jax.ShapeDtypeStruct((rows, cols), BF16)
     large = jax.ShapeDtypeStruct((nrows, cols), BF16)
-    return pl.pallas_call(
+    results = pl.pallas_call(
         functools.partial(kernel, nctx, nhead, group, 2.0 * nrows * cols * nctx * nhead),
         out_shape=(small, small, small, large, large),
         in_specs=[spec] * 7,
@@ -410,10 +422,20 @@
             dma((groups,)),
         ],
         compiler_params=pltpu.CompilerParams(
-            collective_id=0, has_side_effects=True, vmem_limit_bytes=40 * 1024 * 1024
+            collective_id=0, has_side_effects=True, vmem_limit_bytes=63 * 1024 * 1024
         ),
         cost_estimate=pl.CostEstimate(flops=10**9, bytes_accessed=4 * 10**6, transcendentals=10**6),
     )(q_self, k_self, v_self, q_cross, n_keys, n_values, d_cross)
+    return pl.pallas_call(
+        write_out,
+        out_shape=(small, small, small, large, large),
+        in_specs=[spec] * 5,
+        out_specs=(spec,) * 5,
+        scratch_shapes=[pltpu.VMEM((rows, cols), BF16)] * 3
+        + [pltpu.VMEM((nrows, cols), BF16)] * 2
+        + [dma((5,)), dma((5,))],
+        compiler_params=pltpu.CompilerParams(vmem_limit_bytes=63 * 1024 * 1024),
+    )(*results)
 
 
 def solution(mesh):

time: 40.4 us -> 31.9 us (0.79)
  local copies, waits for them, and re-layouts: 10.1 us -> 0 us
  Pallas kernels: 29.3 us -> 31.1 us
    unnamed x19 -> x0, local copies, waits for them, and re-layouts: 10.1 us -> none
    pallas_call x0 -> x1, Pallas kernels: none -> 2.22 us  [body(): pl.pallas_call(write_out, out_shape=(small, small, small, large, large),...]
where the time goes in v2:
time: 31.9 us; the launch traced here: 31.8 us
  Pallas kernels  31.1 us (97%)
  between operations  0.64 us (2%)
    pallas_call x1, Pallas kernels, body(): pl.pallas_call(functools.partial(kernel, nctx, nhead, group, 2.0 * nrows...  28.9 us
    pallas_call x1, Pallas kernels, body(): pl.pallas_call(write_out, out_shape=(small, small, small, large, large),...  2.22 us

profile of v2, /device:TPU:30, one launch (start us, length us, event | category | flops | bytes accessed | tf_op | source)
XLA Modules:
  0.0 31.8 jit_solution(3472938481357725051)
XLA Ops:
  0.6 28.9 %shard_map.110 = (bf16[128,512]{1,0:T(8,128)(2,1)}, bf16[128,512]{1,0:T(8,128)(2,1)}, bf16[128,512]{1,0:T(8,128)(2,1)}, bf16[512,512]{1,0:T(8,128)(2,1)}, bf16[512,512]{1,0:T(8,128)(2,1)}) custom-call(bf16[128,512]{1,0:T(8,128)(2,1)} %q_self.1, bf16[128,512]{1,0:T(8,128)(2,1)} %k_self.1, bf16[128,512]{1,0:T(8,128)(2,1)} %v_self.1, bf16[128,512]{1,0:T(8,128)(2,1)} %q_cross.1, ...), custom_call_target="tpu_custom_call" | custom-call | flops 1000000000 | bytes 4000000 | tf_op jit(solution)/shard_map/pallas_call | solution.py:381
  29.6 2.2 %shard_map.111 = (bf16[128,512]{1,0:T(8,128)(2,1)}, bf16[128,512]{1,0:T(8,128)(2,1)}, bf16[128,512]{1,0:T(8,128)(2,1)}, bf16[512,512]{1,0:T(8,128)(2,1)}, bf16[512,512]{1,0:T(8,128)(2,1)}) custom-call(bf16[128,512]{1,0:T(8,128)(2,1)} %get-tuple-element.10.refs_0_, bf16[128,512]{1,0:T(8,128)(2,1)} %get-tuple-element.11.refs_1_, ...), custom_call_target="tpu_custom_call" | custom-call | tf_op jit(solution)/shard_map/pallas_call | solution.py:429
